TPU v7x, 32 devices: a whole 2x2x4 slice. The times are simulated.
32 devices in a mesh: el: 4 (over x, core), tg: 8 (over z, y).
Axes of the slice: x: 2, y: 2, z: 4, core: 2. Of those that a mesh axis runs over, the one named last changes fastest.
Arguments:
- field_points: bfloat16 [16384, 16, 256], P(('el', 'tg')), may hold values from -6 to 6
- owner_map: int32 [32, 512], P(('el', 'tg')), may hold values from 0 to 31, as said below
- send_counts: int32 [32, 512], P(('el', 'tg')), may hold values from 15 to 16
- tile_rows: int32 [32, 32], P(('el', 'tg')), may hold values from 0 to 31, each once within a row
- tile_cols: int32 [32, 32, 16], P(('el', 'tg')), may hold values from 0 to 63, as said below
- weights: bfloat16 [32, 32, 16, 128, 128], P(('el', 'tg')), may hold values from -0.125 to 0.125
Outputs:
- remapped: bfloat16 [256, 131072], P('el', 'tg')
Inputs may be any that keep to these rules, and one draw needn't show every extreme that they name: `owner_map`: each device's 512 elements name every owner exactly 16 times. `tile_cols`: the 16 entries of one target tile are distinct.
All inputs are finite; a program needn't handle non-finite values.
Results may differ from a plain program's by a relative error of at most 0.001.
Values may be sent and summed in bfloat16 or wider, within the bound.
A program may use at most 128 MiB of HBM per device.

v0:
```python
import jax
import jax.numpy as jnp
from jax import lax
from jax.sharding import PartitionSpec as P


def on_device(field_points, owner_map, send_counts, tile_rows, tile_cols, weights):
    elem_count, point_count, channels = field_points.shape
    devices = lax.axis_size(("el", "tg"))
    per_owner = elem_count // devices
    ordering = jnp.argsort(owner_map[0], stable=True)
    packed = field_points[ordering]
    counts_sorted = send_counts[0][ordering]
    point_index = lax.broadcasted_iota(jnp.int32, (elem_count, point_count), 1)
    live_rows = point_index < counts_sorted[:, None]
    packed = jnp.where(live_rows[:, :, None], packed, jnp.zeros((), packed.dtype))
    outgoing = packed.reshape(devices, per_owner * point_count, channels)
    incoming = lax.all_to_all(outgoing, ("el", "tg"), split_axis=0, concat_axis=0, tiled=True)
    tile_width = weights.shape[-1]
    source = incoming.reshape(-1, tile_width, channels)
    gathered = source[tile_cols[0]]
    product = jnp.einsum("tkij,tkjc->cti", weights[0], gathered, preferred_element_type=jnp.float32)
    placed = jnp.zeros_like(product).at[:, tile_rows[0]].set(product)
    merged = placed.reshape(channels, -1).astype(jnp.bfloat16)
    return lax.all_to_all(merged, "el", split_axis=0, concat_axis=1, tiled=True)


def solution(mesh):
    return jax.shard_map(
        on_device,
        mesh=mesh,
        in_specs=(
            P(("el", "tg"), None, None),
            P(("el", "tg"), None),
            P(("el", "tg"), None),
            P(("el", "tg"), None),
            P(("el", "tg"), None, None),
            P(("el", "tg"), None, None, None, None),
        ),
        out_specs=P("el", "tg"),
        check_vma=False,
    )
```

profile of v0, /device:TPU:0, one launch (start us, length us, event | category | flops | bytes accessed | tf_op | source)
XLA Modules:
  0.0 208.2 jit_solution(14009497301634020718)
XLA Ops:
  0.0 0.0 copy-start
  0.0 4.5 %sort.17 = (s32[512]{0:T(512)}, s32[512]{0:T(512)S(1)}) sort(s32[512]{0:T(512)} %bitcast.33, s32[512]{0:T(512)S(1)} %iota.19), dimensions={0}, to_apply=%region_0.0 | sort | flops 4608 | bytes 8192 | tf_op jit(solution)/shard_map/jit(argsort)/sort | solution.py:11
  4.5 5.1 %gather_fusion.1 = bf16[512,16,256]{2,1,0:T(8,128)(2,1)} fusion(bf16[512,16,256]{2,1,0:T(8,128)(2,1)} %param.6, s32[1024]{0:T(1024)S(1)} %pad_clamp_fusion.1), kind=kCustom, calls=%fused_computation.1 | custom fusion | bytes 8390656 | tf_op jit(solution)/shard_map/gather | solution.py:12
  9.6 0.0 copy-done
  9.6 3.5 %gather_fusion = s32[512]{0:T(512)S(1)} fusion(s32[512]{0:T(512)S(1)} %bitcast.29, s32[1024]{0:T(1024)S(1)} %pad_clamp_fusion.1), kind=kCustom, calls=%fused_computation | custom fusion | bytes 6144 | tf_op jit(solution)/shard_map/gather | solution.py:13
  13.1 0.1 lt.49
  13.2 0.1 copy.12
  13.3 0.1 iota.17
  13.4 0.1 bitcast_compare_fusion
  13.5 0.1 copy.13
  13.6 5.3 %bitcast_select_fusion = bf16[32,256,256]{2,1,0:T(8,128)(2,1)} fusion(pred[32,256]{1,0:T(8,128)(4,1)S(1)} %copy.13, bf16[32,256,256]{2,1,0:T(8,128)(2,1)} %bitcast.31), kind=kLoop, calls=%fused_computation.6 | loop fusion | flops 2097152 | bytes 8396800 | tf_op jit(solution)/shard_map/jit(_where)/select_n | solution.py:16
  18.8 0.0 copy-start.2
  18.8 0.0 copy-start.3
  18.8 7.4 %all-to-all-start = ((bf16[32,256,256]{2,1,0:T(8,128)(2,1)}), bf16[32,256,256]{2,1,0:T(8,128)(2,1)}, u32[]{:S(2)}, u32[]{:S(2)}) async-start(bf16[32,256,256]{2,1,0:T(8,128)(2,1)} %bitcast_select_fusion), calls=%async_computation | async-start | bytes 8388608 | tf_op jit(solution)/shard_map/all_to_all | solution.py:18
  26.3 0.0 copy-done.2
  26.3 0.1 copy.14
  26.4 0.1 reshape.108
  26.4 0.0 copy-done.3
  26.5 95.8 %all-to-all-done = bf16[32,256,256]{2,1,0:T(8,128)(2,1)} async-done(((bf16[32,256,256]{2,1,0:T(8,128)(2,1)}), bf16[32,256,256]{2,1,0:T(8,128)(2,1)}, u32[]{:S(2)}, u32[]{:S(2)}) %all-to-all-start) | async-done | bytes 4194336 | tf_op jit(solution)/shard_map/all_to_all | solution.py:18
  122.2 18.3 %gather_fusion.2 = bf16[512,128,256]{2,1,0:T(8,128)(2,1)} fusion(bf16[64,128,256]{2,1,0:T(8,128)(2,1)} %bitcast.6, s32[1024]{0:T(1024)S(1)} %pad_clamp_fusion), kind=kCustom, calls=%fused_computation.2 | custom fusion | bytes 67110912 | tf_op jit(solution)/shard_map/gather | solution.py:21
  140.5 20.0 %fusion.2 = f32[32,256,128]{2,1,0:T(8,128)} fusion(bf16[32,16,128,256]{3,2,1,0:T(8,128)(2,1)} %bitcast.30, bf16[1,32,16,128,128]{4,3,2,1,0:T(8,128)(2,1)} %param.11), kind=kOutput, calls=%fused_computation.7 | convolution fusion | flops 4294967296 | bytes 54525952 | tf_op jit(solution)/shard_map/tkij,tkjc->cti/dot_general | solution.py:22
  160.5 2.4 %broadcast_in_dim.23 = f32[256,32,128]{2,0,1:T(8,128)} broadcast(f32[]{:T(128)} %constant.6.clone.1), dimensions={} | broadcast | bytes 4194308 | tf_op jit(solution)/shard_map/broadcast_in_dim | solution.py:23
  163.0 8.3 %scatter_fusion = f32[256,32,128]{2,0,1:T(8,128)} fusion(f32[256,32,128]{2,0,1:T(8,128)} %broadcast_in_dim.23, s32[32]{0:T(128)S(1)} %fusion.5, f32[32,256,128]{2,1,0:T(8,128)} %fusion.2), kind=kCustom, calls=%fused_computation.3 | custom fusion | bytes 12583040 | tf_op jit(solution)/shard_map/scatter | solution.py:23
  171.3 2.5 %convert_element_type.7 = bf16[256,32,128]{2,0,1:T(8,128)(2,1)S(1)} convert(f32[256,32,128]{2,0,1:T(8,128)} %scatter_fusion) | non-fusion elementwise | flops 1048576 | bytes 6291456 | tf_op jit(solution)/shard_map/convert_element_type | solution.py:24
  173.8 1.4 copy.16
  175.2 0.0 copy-start.1
  175.2 2.3 %convert_element_type.8 = bf16[4,64,4096]{2,1,0:T(8,128)(2,1)} reshape(bf16[256,32,128]{2,1,0:T(8,128)(2,1)S(1)} %copy.16) | data formatting | bytes 4194304 | tf_op jit(solution)/shard_map/convert_element_type | solution.py:24
  177.5 29.3 %all_to_all.21 = bf16[4,64,4096]{2,1,0:T(8,128)(2,1)S(1)} all-to-all(bf16[4,64,4096]{2,1,0:T(8,128)(2,1)} %convert_element_type.8), channel_id=1, replica_groups=mesh['el'=4,'tg'=8] {'el'}, dimensions={0} | all-to-all | bytes 4194304 | tf_op jit(solution)/shard_map/all_to_all | solution.py:25
  206.7 1.5 copy.20
  208.2 0.0 copy-done.1
  (7 shorter events, 0.0 us)
Async XLA Ops:
  0.0 9.6 %copy-start = (s32[1,512]{1,0:T(1,128)S(1)}, s32[1,512]{1,0:T(1,128)}, u32[]{:S(2)}) copy-start(s32[1,512]{1,0:T(1,128)} %param.8) | copy-start | bytes 6148
  18.8 7.4 %copy-start.2 = (s32[1,32,16]{1,2,0:T(8,128)S(1)}, s32[1,32,16]{1,2,0:T(8,128)}, u32[]{:S(2)}) copy-start(s32[1,32,16]{1,2,0:T(8,128)} %param.10) | copy-start | bytes 6148
  18.8 7.6 %copy-start.3 = (s32[1,32]{1,0:T(1,128)S(1)}, s32[1,32]{1,0:T(1,128)}, u32[]{:S(2)}) copy-start(s32[1,32]{1,0:T(1,128)} %param.9) | copy-start | bytes 388
  18.8 103.4 %all-to-all-start = ((bf16[32,256,256]{2,1,0:T(8,128)(2,1)}), bf16[32,256,256]{2,1,0:T(8,128)(2,1)}, u32[]{:S(2)}, u32[]{:S(2)}) async-start(bf16[32,256,256]{2,1,0:T(8,128)(2,1)} %bitcast_select_fusion), calls=%async_computation | async-start | bytes 8388608 | tf_op jit(solution)/shard_map/all_to_all | solution.py:18
  175.2 33.0 %copy-start.1 = (s32[1,512]{1,0:T(1,128)S(1)}, s32[1,512]{1,0:T(1,128)}, u32[]{:S(2)}) copy-start(s32[1,512]{1,0:T(1,128)} %param.8) | copy-start | bytes 6148
where the time goes:
time: 209 us; the launch traced here: 208 us
  waiting for transfers between devices  95.8 us (46%)
  local copies, waits for them, and re-layouts  43.2 us (21%)
  blocking collectives  29.3 us (14%)
  matrix products  20 us (10%)
  other arithmetic  12.4 us (6%)
  starting transfers between devices  7.43 us (4%)
    all_to_all x1, waiting for transfers between devices, on_device(): lax.all_to_all(outgoing, ('el', 'tg'), split_axis=0, concat_axis=0, tiled...  95.8 us
    all_to_all x1, blocking collectives, on_device(): return lax.all_to_all(merged, 'el', split_axis=0, concat_axis=1, tiled=True)  29.3 us
    dot_general x1, matrix products, on_device(): jnp.einsum('tkij,tkjc->cti', weights[0], gathered, preferred_element_type...  20 us
    gather x1, local copies, waits for them, and re-layouts, on_device(): gathered = source[tile_cols[0]]  18.3 us
    scatter x1, local copies, waits for them, and re-layouts, on_device(): placed = jnp.zeros_like(product).at[:, tile_rows[0]].set(product)  8.32 us
    all_to_all x1, starting transfers between devices, on_device(): lax.all_to_all(outgoing, ('el', 'tg'), split_axis=0, concat_axis=0, tiled...  7.43 us
    select_n x1, other arithmetic, on_device(): jnp.where(live_rows[:, :, None], packed, jnp.zeros((), packed.dtype))  5.25 us
    gather x1, local copies, waits for them, and re-layouts, on_device(): packed = field_points[ordering]  5.13 us
  transfers between devices with their start and end apart: 1, of which 1 were waited for; matrix products, arithmetic and copies ran while one was open for 0% of the time, Pallas kernels for 0%

commit v1 on v0

v1 whole, which is shorter than its diff:
```python
import functools

import jax
import jax.numpy as jnp
from jax import lax
from jax.experimental import pallas as pl
from jax.experimental.pallas import tpu as pltpu
from jax.sharding import PartitionSpec as P

LANES = 128


def kernel(
    n_el, n_tg, per_owner, sel_ref, counts_ref, inv_ref, cols_ref, field_hbm, weights_hbm, out_hbm,
    field, weights, packed, source_far, source_near, mixed, field_sem, weight_sem, own_sem, send_sem, recv_sem,
    swap_send, swap_recv, place_sem,
):
    n = n_el * n_tg
    half_el = n_el // 2
    mesh_id = pl.DeviceIdType.MESH
    my_el = lax.axis_index("el")
    my_tg = lax.axis_index("tg")
    me = my_el * n_tg + my_tg
    points = field.shape[1]
    tiles, blocks = weights.shape[:2]
    tile = weights.shape[2]
    per_half = LANES // half_el
    cells = tiles * tile
    sources = (source_far, source_near)

    field_copy = pltpu.make_async_copy(field_hbm, field, field_sem)
    field_copy.start()
    weight_copy = pltpu.make_async_copy(weights_hbm, weights, weight_sem)

    barrier = pltpu.get_barrier_semaphore()

    def peer(step):
        other = lax.rem(me + step, n)
        return other, (other // n_tg, lax.rem(other, n_tg))

    def greet(step, carry):
        pl.semaphore_signal(barrier, inc=1, device_id=peer(step)[1], device_id_type=mesh_id)
        return carry

    lax.fori_loop(1, n, greet, 0)
    field_copy.wait()

    row = lax.broadcasted_iota(jnp.int32, (points, LANES), 0)

    def pack(other):
        def one(g, carry):
            element = sel_ref[other * per_owner + g]
            live = row < counts_ref[element]
            for h in range(2):
                values = field[element, :, h * LANES:(h + 1) * LANES]
                packed[h, other, g] = jnp.where(live, values, jnp.zeros_like(values))
            return carry

        lax.fori_loop(0, per_owner, one, 0, unroll=min(per_owner, 4))

    def lanes_of(other_el, phase):
        near = other_el // half_el
        return 1 - near if phase == 0 else near

    def send(step, phase):
        other, where = peer(step)
        return pltpu.make_async_remote_copy(
            src_ref=packed.at[lanes_of(where[0], phase), other],
            dst_ref=sources[phase].at[me],
            send_sem=send_sem.at[phase, step],
            recv_sem=recv_sem.at[phase, step],
            device_id=where,
            device_id_type=mesh_id,
        )

    def arrival(step, phase):
        sender = lax.rem(me + n - step, n)
        return pltpu.make_async_copy(packed.at[0, 0], sources[phase].at[sender], recv_sem.at[phase, step])

    pack(lax.rem(me + 1, n))
    pl.semaphore_wait(barrier, n - 1)

    def first(step, carry):
        send(step, 0).start()
        pack(lax.rem(me + step + 1, n))
        return carry

    lax.fori_loop(1, n, first, 0)
    weight_copy.start()
    for phase in range(2):
        pltpu.make_async_copy(packed.at[lanes_of(my_el, phase), me], sources[phase].at[me], own_sem.at[phase]).start()

    def second(step, carry):
        send(step, 0).wait_send()
        send(step, 1).start()
        return carry

    lax.fori_loop(1, n, second, 0)

    def multiply(phase):
        def landed(step, carry):
            arrival(step, phase).wait()
            return carry

        lax.fori_loop(1, n, landed, 0)
        pltpu.make_async_copy(packed.at[0, 0], sources[phase].at[me], own_sem.at[phase]).wait()
        flat = sources[phase].reshape(n * per_owner * points // tile, tile, LANES)

        def one(q, carry):
            t = inv_ref[q]
            left = jnp.concatenate([weights[t, k] for k in range(blocks)], axis=1)
            right = jnp.concatenate([flat[cols_ref[t * blocks + k]] for k in range(blocks)], axis=0)
            product = jnp.dot(left, right, preferred_element_type=jnp.float32)
            start = pl.multiple_of(q * tile, tile)
            mixed[phase, :, pl.ds(start, tile)] = product.T.astype(mixed.dtype)
            return carry

        lax.fori_loop(0, tiles, one, 0)

    my_columns = pl.ds(pl.multiple_of(my_el * cells, cells), cells)
    my_half = my_el // half_el

    def swap(phase, m):
        group = 1 - my_half if phase == 0 else my_half
        index = lax.rem(lax.rem(my_el, half_el) + m, half_el)
        return pltpu.make_async_remote_copy(
            src_ref=mixed.at[phase, pl.ds(pl.multiple_of(index * per_half, per_half), per_half)],
            dst_ref=out_hbm.at[:, my_columns],
            send_sem=swap_send.at[phase, m],
            recv_sem=swap_recv.at[phase, m],
            device_id=(group * half_el + index, my_tg),
            device_id_type=mesh_id,
        )

    def swapped(phase, m):
        group = 1 - my_half if phase == 0 else my_half
        index = lax.rem(lax.rem(my_el, half_el) + half_el - m, half_el)
        columns = pl.ds(pl.multiple_of((group * half_el + index) * cells, cells), cells)
        return pltpu.make_async_copy(
            mixed.at[phase, pl.ds(0, per_half)], out_hbm.at[:, columns], swap_recv.at[phase, m]
        )

    weight_copy.wait()
    multiply(0)
    for m in range(half_el):
        swap(0, m).start()
    multiply(1)
    for m in range(1, half_el):
        swap(1, m).start()
    mine = pl.multiple_of(lax.rem(my_el, half_el) * per_half, per_half)
    place = pltpu.make_async_copy(mixed.at[1, pl.ds(mine, per_half)], out_hbm.at[:, my_columns], place_sem)
    place.start()

    def sent(step, carry):
        send(step, 1).wait_send()
        return carry

    lax.fori_loop(1, n, sent, 0)
    for phase in range(2):
        for m in range(phase, half_el):
            swap(phase, m).wait_send()
            swapped(phase, m).wait()
    place.wait()


def on_device(n_el, n_tg, field_points, owner_map, send_counts, tile_rows, tile_cols, weights):
    elements, points, channels = field_points.shape
    n = n_el * n_tg
    per_owner = elements // n
    _, tiles, blocks, tile, _ = weights.shape
    owner = owner_map[0]
    index = jnp.arange(elements, dtype=jnp.int32)
    same = (owner[:, None] == owner[None, :]) & (index[None, :] < index[:, None])
    slot = owner * per_owner + jnp.sum(same.astype(jnp.int32), axis=1)
    sel = jnp.sum(jnp.where(slot[:, None] == index[None, :], index[:, None], 0), axis=0)
    order = jnp.arange(tiles, dtype=jnp.int32)
    inverse = jnp.sum(jnp.where(tile_rows[0][:, None] == order[None, :], order[:, None], 0), axis=0)
    half_el = n_el // 2
    smem = pl.BlockSpec(memory_space=pltpu.SMEM)
    anywhere = pl.BlockSpec(memory_space=pl.ANY)
    dma = pltpu.SemaphoreType.DMA
    kind = field_points.dtype
    return pl.pallas_call(
        functools.partial(kernel, n_el, n_tg, per_owner),
        out_shape=jax.ShapeDtypeStruct((channels // n_el, n_el * tiles * tile), kind),
        in_specs=[smem] * 4 + [anywhere] * 2,
        out_specs=anywhere,
        scratch_shapes=[
            pltpu.VMEM((elements, points, channels), kind),
            pltpu.VMEM((tiles, blocks, tile, tile), kind),
            pltpu.VMEM((2, n, per_owner, points, LANES), kind),
            pltpu.VMEM((n, per_owner, points, LANES), kind),
            pltpu.VMEM((n, per_owner, points, LANES), kind),
            pltpu.VMEM((2, LANES, tiles * tile), kind),
            dma(()),
            dma(()),
            dma((2,)),
            dma((2, n)),
            dma((2, n)),
            dma((2, half_el)),
            dma((2, half_el)),
            dma(()),
        ],
        compiler_params=pltpu.CompilerParams(
            collective_id=0, has_side_effects=True, vmem_limit_bytes=56 * 2**20
        ),
        cost_estimate=pl.CostEstimate(
            flops=2 * tiles * blocks * tile * tile * channels,
            bytes_accessed=weights.size * 2 + field_points.size * 2,
            transcendentals=0,
        ),
    )(sel, send_counts[0], inverse, tile_cols[0].reshape(-1), field_points, weights[0])


def solution(mesh):
    n_el, n_tg = mesh.shape["el"], mesh.shape["tg"]
    return jax.shard_map(
        functools.partial(on_device, n_el, n_tg),
        mesh=mesh,
        in_specs=(
            P(("el", "tg"), None, None),
            P(("el", "tg"), None),
            P(("el", "tg"), None),
            P(("el", "tg"), None),
            P(("el", "tg"), None, None),
            P(("el", "tg"), None, None, None, None),
        ),
        out_specs=P("el", "tg"),
        check_vma=False,
    )
```

time: 209 us -> 123 us (0.59)
  the two profiles are of different devices: /device:TPU:0 before, /device:TPU:13 now
where the time goes in v1:
time: 123 us; the launch traced here: 121 us
  Pallas kernels  113 us (92%)
  local copies, waits for them, and re-layouts  4.49 us (4%)
  other arithmetic  3.74 us (3%)
    pallas_call x1, Pallas kernels, on_device(): pl.pallas_call(functools.partial(kernel, n_el, n_tg, per_owner), out_shap...  113 us
    unnamed x2, local copies, waits for them, and re-layouts  3.81 us

profile of v1, /device:TPU:13, one launch (start us, length us, event | category | flops | bytes accessed | tf_op | source)
XLA Modules:
  0.0 121.4 jit_solution(10665130527067653483)
XLA Ops:
  0.0 1.3 %select_reduce_fusion.1.inv_ref = s32[32]{0:T(128)} fusion(s32[32]{0:T(128)} %bitcast.8), kind=kLoop, calls=%fused_computation.5 | loop fusion | flops 3040 | bytes 256 | tf_op jit(solution)/shard_map/reduce_sum | solution.py:177
  1.3 1.0 convert_reduce_fusion
  2.3 0.7 multiply_add_fusion
  3.0 0.8 select_reduce_fusion.sel_ref
  3.7 0.8 copy.8
  4.5 0.7 reshape_squeeze.3.cols_ref
  5.2 113.1 %shard_map.64 = bf16[64,16384]{1,0:T(8,128)(2,1)} custom-call(s32[512]{0:T(512)} %select_reduce_fusion.sel_ref, s32[512]{0:T(512)} %bitcast.7, s32[32]{0:T(128)} %select_reduce_fusion.1.inv_ref, s32[512]{0:T(512)} %reshape_squeeze.3.cols_ref, bf16[512,16,256]{2,1,0:T(8,128)(2,1)} %field_hbm.1, bf16[32,16,128,128]{3,2,1,0:T(8,128)(2,1)} %bitcast.4), custom_call_target="tpu_custom_call" | custom-call | flops 4294967296 | bytes 20971520 | tf_op jit(solution)/shard_map/pallas_call | solution.py:183
  118.3 3.0 %copy.10 = bf16[64,16384]{1,0:T(8,128)(2,1)} copy(bf16[64,16384]{1,0:T(8,128)(2,1)} %shard_map.64) | data formatting | bytes 4194304

commit v2 on v1

v2 whole, which is shorter than its diff:
```python
import functools

import jax
import jax.numpy as jnp
from jax import lax
from jax.experimental import pallas as pl
from jax.experimental.pallas import tpu as pltpu
from jax.sharding import PartitionSpec as P

LANES = 128
GROUPS = 4
UNROLL = 2


def kernel(
    n_el, n_tg, per_owner, owner_ref, counts_ref, rows_ref, cols_ref, field_hbm, weights_hbm, out_hbm,
    field, weights, packed, source_far, source_near, mixed, field_sem, weight_sem, own_sem, send_sem, recv_sem,
    swap_send, swap_recv, place_sem, table_vmem, place_vmem, table, place_table, table_sem,
):
    n = n_el * n_tg
    half_el = n_el // 2
    mesh_id = pl.DeviceIdType.MESH
    my_el = lax.axis_index("el")
    my_tg = lax.axis_index("tg")
    me = my_el * n_tg + my_tg
    points = field.shape[1]
    tiles, blocks = weights.shape[:2]
    tile = weights.shape[2]
    per_half = LANES // half_el
    cells = tiles * tile
    sources = (source_far, source_near)

    field_copy = pltpu.make_async_copy(field_hbm, field, field_sem)
    field_copy.start()
    weight_copy = pltpu.make_async_copy(weights_hbm, weights, weight_sem)

    barrier = pltpu.get_barrier_semaphore()

    def offsets(step):
        count = step + 1
        return lax.rem(count // n_tg, n_el), lax.rem(count, n_tg)

    def peer(step):
        el_step, tg_step = offsets(step)
        where = (lax.rem(my_el + el_step, n_el), lax.rem(my_tg + tg_step, n_tg))
        return where[0] * n_tg + where[1], where

    def greet(step, carry):
        pl.semaphore_signal(barrier, inc=1, device_id=peer(step)[1], device_id_type=mesh_id)
        return carry

    lax.fori_loop(0, n - 1, greet, 0)

    slots = table_vmem.shape[0] // 2
    elements = field.shape[0]
    owner = owner_ref[...]
    index = lax.broadcasted_iota(jnp.int32, (1, elements), 1)
    owned = lax.broadcasted_iota(jnp.int32, (table_vmem.shape[1], elements), 0) == owner
    onehot = owned.astype(jnp.float32).astype(jnp.bfloat16)
    earlier = lax.broadcasted_iota(jnp.int32, (elements, elements), 0) < lax.broadcasted_iota(
        jnp.int32, (elements, elements), 1
    )
    before = jnp.dot(onehot, earlier.astype(jnp.float32).astype(jnp.bfloat16), preferred_element_type=jnp.float32)
    rank = jnp.sum(jnp.where(owned, before, 0.0), axis=0, keepdims=True).astype(jnp.int32)
    ranked = lax.broadcasted_iota(jnp.int32, (slots, elements), 0) == rank
    picks = [jnp.where(ranked, x, 0).astype(jnp.float32) for x in (index // LANES, lax.rem(index, LANES), counts_ref[...])]
    found = lax.dot_general(
        jnp.concatenate(picks, axis=0).astype(jnp.bfloat16), onehot, (((1,), (1,)), ((), ())),
        preferred_element_type=jnp.float32,
    ).astype(jnp.int32)
    table_vmem[:slots] = found[:slots] * LANES + found[slots:2 * slots]
    table_vmem[slots:] = found[2 * slots:]
    placed = lax.broadcasted_iota(jnp.int32, (place_vmem.shape[1], tiles), 0) == rows_ref[...]
    order = lax.broadcasted_iota(jnp.int32, (place_vmem.shape[0], tiles), 1)
    place_vmem[...] = lax.dot_general(
        order.astype(jnp.float32).astype(jnp.bfloat16), placed.astype(jnp.float32).astype(jnp.bfloat16),
        (((1,), (1,)), ((), ())), preferred_element_type=jnp.float32,
    ).astype(jnp.int32)
    table_copies = [
        pltpu.make_async_copy(table_vmem, table, table_sem.at[0]),
        pltpu.make_async_copy(place_vmem, place_table, table_sem.at[1]),
    ]
    for copy in table_copies:
        copy.start()
    for copy in table_copies:
        copy.wait()
    field_copy.wait()

    row = lax.broadcasted_iota(jnp.int32, (points, LANES), 0)

    def pack(other):
        def one(g, carry):
            element = jnp.clip(table[g, other], 0, elements - 1)
            live = row < table[slots + g, other]
            for h in range(2):
                values = field[element, :, h * LANES:(h + 1) * LANES]
                packed[h, other, g] = jnp.where(live, values, jnp.zeros_like(values))
            return carry

        lax.fori_loop(0, per_owner, one, 0, unroll=min(per_owner, 4))

    def lanes_of(other_el, phase):
        near = other_el // half_el
        return 1 - near if phase == 0 else near

    def send(step, phase):
        other, where = peer(step)
        return pltpu.make_async_remote_copy(
            src_ref=packed.at[lanes_of(where[0], phase), other],
            dst_ref=sources[phase].at[me],
            send_sem=send_sem.at[phase, step],
            recv_sem=recv_sem.at[phase, step],
            device_id=where,
            device_id_type=mesh_id,
        )

    def arrival(step, phase):
        el_step, tg_step = offsets(step)
        sender = lax.rem(my_el + n_el - el_step, n_el) * n_tg + lax.rem(my_tg + n_tg - tg_step, n_tg)
        return pltpu.make_async_copy(packed.at[0, 0], sources[phase].at[sender], recv_sem.at[phase, step])

    pack(peer(0)[0])
    pl.semaphore_wait(barrier, n - 1)

    def first(step, carry):
        send(step, 0).start()
        pack(peer(step + 1)[0])
        return carry

    lax.fori_loop(0, n - 1, first, 0)
    weight_copy.start()
    for phase in range(2):
        pltpu.make_async_copy(packed.at[lanes_of(my_el, phase), me], sources[phase].at[me], own_sem.at[phase]).start()

    def second(step, carry):
        send(step, 0).wait_send()
        send(step, 1).start()
        return carry

    lax.fori_loop(0, n - 1, second, 0)

    def land(phase):
        def landed(step, carry):
            arrival(step, phase).wait()
            return carry

        lax.fori_loop(0, n - 1, landed, 0)
        pltpu.make_async_copy(packed.at[0, 0], sources[phase].at[me], own_sem.at[phase]).wait()

    def multiply(phase, group):
        flat = sources[phase].reshape(n * per_owner * points // tile, tile, LANES)

        def one(q, carry):
            t = jnp.clip(place_table[0, q], 0, tiles - 1)
            left = jnp.concatenate([weights[t, k] for k in range(blocks)], axis=1)
            right = jnp.concatenate([flat[cols_ref[k, t]] for k in range(blocks)], axis=0)
            product = jnp.dot(left, right, preferred_element_type=jnp.float32)
            start = pl.multiple_of(q * tile, tile)
            mixed[phase, :, pl.ds(start, tile)] = product.T.astype(mixed.dtype)
            return carry

        share = tiles // GROUPS
        lax.fori_loop(group * share, (group + 1) * share, one, 0, unroll=UNROLL)

    piece = cells // GROUPS
    my_half = my_el // half_el
    my_index = lax.rem(my_el, half_el)

    def block(index):
        return pl.ds(pl.multiple_of(index * per_half, per_half), per_half)

    def columns(owner_el, group):
        return pl.ds(pl.multiple_of(owner_el * cells + group * piece, piece), piece)

    def swap(phase, m, group):
        side = 1 - my_half if phase == 0 else my_half
        index = lax.rem(my_index + m, half_el)
        return pltpu.make_async_remote_copy(
            src_ref=mixed.at[phase, block(index), pl.ds(group * piece, piece)],
            dst_ref=out_hbm.at[:, columns(my_el, group)],
            send_sem=swap_send.at[phase, m, group],
            recv_sem=swap_recv.at[phase, m, group],
            device_id=(side * half_el + index, my_tg),
            device_id_type=mesh_id,
        )

    def swapped(phase, m, group):
        side = 1 - my_half if phase == 0 else my_half
        index = lax.rem(my_index + half_el - m, half_el)
        return pltpu.make_async_copy(
            mixed.at[phase, pl.ds(0, per_half), pl.ds(group * piece, piece)],
            out_hbm.at[:, columns(side * half_el + index, group)],
            swap_recv.at[phase, m, group],
        )

    def place(group):
        return pltpu.make_async_copy(
            mixed.at[1, block(my_index), pl.ds(group * piece, piece)],
            out_hbm.at[:, columns(my_el, group)],
            place_sem.at[group],
        )

    weight_copy.wait()
    for phase in range(2):
        land(phase)
        for group in range(GROUPS):
            multiply(phase, group)
            for m in range(phase, half_el):
                swap(phase, m, group).start()
            if phase == 1:
                place(group).start()

    def sent(step, carry):
        send(step, 1).wait_send()
        return carry

    lax.fori_loop(0, n - 1, sent, 0)
    for group in range(GROUPS):
        for phase in range(2):
            for m in range(phase, half_el):
                swap(phase, m, group).wait_send()
                swapped(phase, m, group).wait()
        place(group).wait()


def on_device(n_el, n_tg, field_points, owner_map, send_counts, tile_rows, tile_cols, weights):
    elements, points, channels = field_points.shape
    n = n_el * n_tg
    per_owner = elements // n
    _, tiles, blocks, tile, _ = weights.shape
    half_el = n_el // 2
    smem = pl.BlockSpec(memory_space=pltpu.SMEM)
    vmem = pl.BlockSpec(memory_space=pltpu.VMEM)
    slots = max(16, per_owner)
    anywhere = pl.BlockSpec(memory_space=pl.ANY)
    dma = pltpu.SemaphoreType.DMA
    kind = field_points.dtype
    return pl.pallas_call(
        functools.partial(kernel, n_el, n_tg, per_owner),
        out_shape=jax.ShapeDtypeStruct((channels // n_el, n_el * tiles * tile), kind),
        in_specs=[vmem] * 3 + [smem] + [anywhere] * 2,
        out_specs=anywhere,
        scratch_shapes=[
            pltpu.VMEM((elements, points, channels), kind),
            pltpu.VMEM((tiles, blocks, tile, tile), kind),
            pltpu.VMEM((2, n, per_owner, points, LANES), kind),
            pltpu.VMEM((n, per_owner, points, LANES), kind),
            pltpu.VMEM((n, per_owner, points, LANES), kind),
            pltpu.VMEM((2, LANES, tiles * tile), kind),
            dma(()),
            dma(()),
            dma((2,)),
            dma((2, n)),
            dma((2, n)),
            dma((2, half_el, GROUPS)),
            dma((2, half_el, GROUPS)),
            dma((GROUPS,)),
            pltpu.VMEM((2 * slots, max(n, LANES)), jnp.int32),
            pltpu.VMEM((8, LANES), jnp.int32),
            pltpu.SMEM((2 * slots, max(n, LANES)), jnp.int32),
            pltpu.SMEM((8, LANES), jnp.int32),
            dma((2,)),
        ],
        compiler_params=pltpu.CompilerParams(
            collective_id=0, has_side_effects=True, vmem_limit_bytes=56 * 2**20
        ),
        cost_estimate=pl.CostEstimate(
            flops=2 * tiles * blocks * tile * tile * channels,
            bytes_accessed=weights.size * 2 + field_points.size * 2,
            transcendentals=0,
        ),
    )(owner_map, send_counts, tile_rows, tile_cols[0].T, field_points, weights[0])


def solution(mesh):
    n_el, n_tg = mesh.shape["el"], mesh.shape["tg"]
    return jax.shard_map(
        functools.partial(on_device, n_el, n_tg),
        mesh=mesh,
        in_specs=(
            P(("el", "tg"), None, None),
            P(("el", "tg"), None),
            P(("el", "tg"), None),
            P(("el", "tg"), None),
            P(("el", "tg"), None, None),
            P(("el", "tg"), None, None, None, None),
        ),
        out_specs=P("el", "tg"),
        check_vma=False,
    )
```

time: 123 us -> 113 us (0.919)
  Pallas kernels: 113 us -> 109 us
  other arithmetic: 3.74 us -> 0 us
  local copies, waits for them, and re-layouts: 4.49 us -> 3.05 us
    pallas_call x1, Pallas kernels: 113 us -> 109 us  [on_device(): pl.pallas_call(functools.partial(kernel, n_el, n_tg, per_owner), out_shap...]
    reduce_sum x3 -> x0, other arithmetic: 3.05 us -> none  [the longest x1 1.28 us: on_device(): jnp.sum(jnp.where(tile_rows[0][:, None] == order[None, :], order[:, None]...]
    unnamed x2 -> x1, local copies, waits for them, and re-layouts: 3.81 us -> 3.05 us
where the time goes in v2:
time: 113 us; the launch traced here: 112 us
  Pallas kernels  109 us (96%)
  local copies, waits for them, and re-layouts  3.05 us (3%)
    pallas_call x1, Pallas kernels, on_device(): pl.pallas_call(functools.partial(kernel, n_el, n_tg, per_owner), out_shap...  109 us
    unnamed x1, local copies, waits for them, and re-layouts  3.05 us

profile of v2, /device:TPU:13, one launch (start us, length us, event | category | flops | bytes accessed | tf_op | source)
XLA Modules:
  0.0 112.3 jit_solution(12759196925299771547)
XLA Ops:
  0.0 109.3 %shard_map.64 = bf16[64,16384]{1,0:T(8,128)(2,1)} custom-call(s32[1,512]{1,0:T(1,128)} %owner_ref.1, s32[1,512]{1,0:T(1,128)} %counts_ref.1, s32[1,32]{1,0:T(1,128)} %rows_ref.1, s32[16,32]{1,0:T(8,128)} %bitcast.5, bf16[512,16,256]{2,1,0:T(8,128)(2,1)} %field_hbm.1, bf16[32,16,128,128]{3,2,1,0:T(8,128)(2,1)} %bitcast.4), custom_call_target="tpu_custom_call" | custom-call | flops 4294967296 | bytes 20971520 | tf_op jit(solution)/shard_map/pallas_call | solution.py:238
  109.3 3.0 %copy.8 = bf16[64,16384]{1,0:T(8,128)(2,1)} copy(bf16[64,16384]{1,0:T(8,128)(2,1)} %shard_map.64) | data formatting | bytes 4194304

commit v3 on v2

--- a/solution.py
+++ b/solution.py
@@ -9,7 +9,7 @@
 
 LANES = 128
 GROUPS = 4
-UNROLL = 2
+UNROLL = 4
 
 
 def kernel(
@@ -237,9 +237,9 @@
     kind = field_points.dtype
     return pl.pallas_call(
         functools.partial(kernel, n_el, n_tg, per_owner),
-        out_shape=jax.ShapeDtypeStruct((channels // n_el, n_el * tiles * tile), kind),
+        out_shape=pltpu.VMEM((channels // n_el, n_el * tiles * tile), kind),
         in_specs=[vmem] * 3 + [smem] + [anywhere] * 2,
-        out_specs=anywhere,
+        out_specs=vmem,
         scratch_shapes=[
             pltpu.VMEM((elements, points, channels), kind),
             pltpu.VMEM((tiles, blocks, tile, tile), kind),

time: 113 us -> 110 us (0.973)
  local copies, waits for them, and re-layouts: 3.05 us -> 1.32 us
    unnamed x1, local copies, waits for them, and re-layouts: 3.05 us -> 1.32 us
where the time goes in v3:
time: 110 us
  Pallas kernels  109 us (99%)
  local copies, waits for them, and re-layouts  1.32 us (1%)
    pallas_call x1, Pallas kernels, on_device(): pl.pallas_call(functools.partial(kernel, n_el, n_tg, per_owner), out_shap...  109 us

profile of v3, /device:TPU:13, one launch (start us, length us, event | category | flops | bytes accessed | tf_op | source)
XLA Modules:
  0.0 110.1 jit_solution(11182089351882111611)
XLA Ops:
  0.0 108.7 %shard_map.64 = bf16[64,16384]{1,0:T(8,128)(2,1)S(1)} custom-call(s32[1,512]{1,0:T(1,128)} %owner_ref.1, s32[1,512]{1,0:T(1,128)} %counts_ref.1, s32[1,32]{1,0:T(1,128)} %rows_ref.1, s32[16,32]{1,0:T(8,128)} %bitcast.5, bf16[512,16,256]{2,1,0:T(8,128)(2,1)} %field_hbm.1, bf16[32,16,128,128]{3,2,1,0:T(8,128)(2,1)} %bitcast.4), custom_call_target="tpu_custom_call" | custom-call | flops 4294967296 | bytes 20971520 | tf_op jit(solution)/shard_map/pallas_call | solution.py:238
  108.7 1.3 %copy.8 = bf16[64,16384]{1,0:T(8,128)(2,1)} copy(bf16[64,16384]{1,0:T(8,128)(2,1)S(1)} %shard_map.64) | data formatting | bytes 4194304
